TPU v7x, 32 devices: a whole 2x2x4 slice. The times are simulated.
32 devices in a mesh: dp: 16 (over z, y, x), seq: 2 (over core).
Axes of the slice: x: 2, y: 2, z: 4, core: 2. Of those that a mesh axis runs over, the one named last changes fastest.
Arguments:
- patches: bfloat16 [64, 544, 768], P('dp', 'seq'), may hold values from -6 to 6
- lengths: int32 [64], P('dp'), may hold values from 40 to 529, as said below
- gain_one: float32 [768], replicated, may hold values from 0.5 to 1.5
- shift_one: float32 [768], replicated, may hold values from -2 to 2
- w_query: bfloat16 [768, 768], replicated, may hold values from -0.21875 to 0.21875
- b_query: float32 [768], replicated, may hold values from -2 to 2
- w_key: bfloat16 [768, 768], replicated, may hold values from -0.21875 to 0.21875
- w_value: bfloat16 [768, 768], replicated, may hold values from -0.21875 to 0.21875
- b_value: float32 [768], replicated, may hold values from -2 to 2
- w_out: bfloat16 [768, 768], replicated, may hold values from -1.75 to 1.75
- b_out: float32 [768], replicated, may hold values from -2 to 2
- gain_two: float32 [768], replicated, may hold values from 0.5 to 1.5
- shift_two: float32 [768], replicated, may hold values from -2 to 2
- w_up: bfloat16 [768, 3072], replicated, may hold values from -0.21875 to 0.21875
- b_up: float32 [3072], replicated, may hold values from -2 to 2
- w_down: bfloat16 [3072, 768], replicated, may hold values from -0.109375 to 0.109375
- b_down: float32 [768], replicated, may hold values from -2 to 2
- cotangent: bfloat16 [64, 544, 768], P('dp', 'seq'), may hold values from -6 to 6
Outputs:
- output: bfloat16 [64, 544, 768], P('dp', 'seq')
- grad_patches: bfloat16 [64, 544, 768], P('dp', 'seq')
- grad_gain_one: float32 [768], replicated
- grad_shift_one: float32 [768], replicated
- grad_w_query: float32 [768, 768], replicated
- grad_b_query: float32 [768], replicated
- grad_w_key: float32 [768, 768], replicated
- grad_w_value: float32 [768, 768], replicated
- grad_b_value: float32 [768], replicated
- grad_w_out: float32 [768, 768], replicated
- grad_b_out: float32 [768], replicated
- grad_gain_two: float32 [768], replicated
- grad_shift_two: float32 [768], replicated
- grad_w_up: float32 [768, 3072], replicated
- grad_b_up: float32 [3072], replicated
- grad_w_down: float32 [3072, 768], replicated
- grad_b_down: float32 [768], replicated
Inputs may be any that keep to these rules, and one draw needn't show every extreme that they name: `lengths`: in each aligned block of 4 strips one strip has exactly 529 valid patches; valid patches come first in a strip.
All inputs are finite; a program needn't handle non-finite values.
Results may differ from a plain program's by a relative error of at most 0.012.
Values may be sent and summed in bfloat16 or wider, within the bound.
No kernel may reach another device: no remote copies, remote signals or barrier semaphores. Data moves between devices by JAX's collectives and lax.ppermute only.
A program may use at most 256 MiB of HBM per device.

v0:
```python
import jax
import jax.numpy as jnp
from jax import lax
from jax.sharding import PartitionSpec as P

HEAD_DIM = 64
epsilon = 1e-06


def exact_gelu(values):
    return jax.nn.gelu(values, approximate=False)


def project(left_rows, weight):
    return jnp.dot(left_rows, weight, preferred_element_type=jnp.float32)


def project_back(grad_rows, weight):
    return jnp.einsum("stf,df->std", grad_rows, weight, preferred_element_type=jnp.float32)


def weight_grad(left_rows, grad_rows):
    return jnp.einsum("std,stf->df", left_rows, grad_rows, preferred_element_type=jnp.float32)


def column_sums(grad_rows):
    return jnp.sum(grad_rows.astype(jnp.float32), axis=(0, 1))


def norm_forward(values, gain, shift):
    centre = jnp.mean(values, axis=-1, keepdims=True)
    centred = values - centre
    spread = jnp.mean(centred * centred, axis=-1, keepdims=True)
    rstd_rows = lax.rsqrt(spread + epsilon)
    scaled = centred * rstd_rows
    return ((scaled * gain + shift).astype(jnp.bfloat16), scaled, rstd_rows)


def norm_backward(grad_out, scaled, rstd_rows, gain):
    weighted = grad_out * gain
    mean_grad = jnp.mean(weighted, axis=-1, keepdims=True)
    mean_cross = jnp.mean(weighted * scaled, axis=-1, keepdims=True)
    grad_in = rstd_rows * (weighted - mean_grad - scaled * mean_cross)
    return (grad_in, jnp.sum(grad_out * scaled, axis=(0, 1)), jnp.sum(grad_out, axis=(0, 1)))


def split_heads(block_rows):
    return block_rows.reshape(block_rows.shape[0], block_rows.shape[1] // HEAD_DIM, HEAD_DIM)


def masked_scores(query_heads, key_heads, length):
    score_scale = HEAD_DIM ** (-0.5)
    scores = (
        jnp.einsum("qhd,khd->hqk", query_heads, key_heads, preferred_element_type=jnp.float32)
        * score_scale
    )
    key_valid = lax.iota(jnp.int32, key_heads.shape[0]) < length
    return jnp.where(key_valid[None, None, :], scores, -jnp.inf)


def attend(block_item):
    query_block, key_block, value_block, length = block_item
    value_heads = split_heads(value_block)
    scores = masked_scores(split_heads(query_block), split_heads(key_block), length)
    row_max = jnp.max(scores, axis=-1, keepdims=True)
    exponent = jnp.exp(scores - row_max)
    row_total = jnp.sum(exponent, axis=-1, keepdims=True)
    attn_probs = (exponent / row_total).astype(jnp.bfloat16)
    log_total = (row_max + jnp.log(row_total))[..., 0]
    context_rows = jnp.einsum(
        "hqk,khd->qhd", attn_probs, value_heads, preferred_element_type=jnp.float32
    )
    return (context_rows.reshape(context_rows.shape[0], -1).astype(jnp.bfloat16), log_total)


def attend_back(block_item):
    query_block, key_block, value_block, grad_block, log_total, length = block_item
    score_scale = HEAD_DIM ** (-0.5)
    query_heads = split_heads(query_block)
    key_heads = split_heads(key_block)
    value_heads = split_heads(value_block)
    grad_heads = split_heads(grad_block)
    scores = masked_scores(query_heads, key_heads, length)
    probs_exact = jnp.exp(scores - log_total[:, :, None])
    attn_probs = probs_exact.astype(jnp.bfloat16)
    grad_values = jnp.einsum(
        "hqk,qhd->khd", attn_probs, grad_heads, preferred_element_type=jnp.float32
    )
    grad_probs = jnp.einsum(
        "qhd,khd->hqk", grad_heads, value_heads, preferred_element_type=jnp.float32
    )
    inner = jnp.sum(grad_probs * probs_exact, axis=-1, keepdims=True)
    grad_scores = (probs_exact * (grad_probs - inner)).astype(jnp.bfloat16)
    grad_queries = (
        jnp.einsum("hqk,khd->qhd", grad_scores, key_heads, preferred_element_type=jnp.float32)
        * score_scale
    )
    grad_keys = (
        jnp.einsum("hqk,qhd->khd", grad_scores, query_heads, preferred_element_type=jnp.float32)
        * score_scale
    )
    slots = query_block.shape[0]
    return (
        grad_queries.reshape(slots, -1).astype(jnp.bfloat16),
        grad_keys.reshape(slots, -1).astype(jnp.bfloat16),
        grad_values.reshape(slots, -1).astype(jnp.bfloat16),
    )


def local(
    patches,
    lengths,
    gain_one,
    shift_one,
    w_query,
    b_query,
    w_key,
    w_value,
    b_value,
    w_out,
    b_out,
    gain_two,
    shift_two,
    w_up,
    b_up,
    w_down,
    b_down,
    cotangent,
):
    inputs = patches.astype(jnp.float32)
    normed_one, scaled_one, rstd_one = norm_forward(inputs, gain_one, shift_one)
    queries = (project(normed_one, w_query) + b_query).astype(jnp.bfloat16)
    key_rows = project(normed_one, w_key).astype(jnp.bfloat16)
    value_rows = (project(normed_one, w_value) + b_value).astype(jnp.bfloat16)
    query_whole, key_whole, value_whole = (
        lax.all_to_all(queries, "seq", split_axis=2, concat_axis=1, tiled=True),
        lax.all_to_all(key_rows, "seq", split_axis=2, concat_axis=1, tiled=True),
        lax.all_to_all(value_rows, "seq", split_axis=2, concat_axis=1, tiled=True),
    )
    context_whole, log_totals = lax.map(attend, (query_whole, key_whole, value_whole, lengths))
    context = lax.all_to_all(context_whole, "seq", split_axis=1, concat_axis=2, tiled=True)
    hidden = inputs + project(context, w_out) + b_out
    normed_two, scaled_two, rstd_two = norm_forward(hidden, gain_two, shift_two)
    upper_pre = project(normed_two, w_up) + b_up
    active = exact_gelu(upper_pre).astype(jnp.bfloat16)
    output = (hidden + project(active, w_down) + b_down).astype(jnp.bfloat16)
    grad_y = cotangent.astype(jnp.float32)
    g_down = weight_grad(active, cotangent)
    g_bdown = jnp.sum(grad_y, axis=(0, 1))
    grad_active = project_back(cotangent, w_down)
    unused_value, gelu_pull = jax.vjp(exact_gelu, upper_pre)
    grad_upper = gelu_pull(grad_active)[0].astype(jnp.bfloat16)
    g_up = weight_grad(normed_two, grad_upper)
    g_bup = column_sums(grad_upper)
    grad_normed_two = project_back(grad_upper, w_up)
    grad_from_two, g_gain_two, g_shift_two = norm_backward(
        grad_normed_two, scaled_two, rstd_two, gain_two
    )
    grad_hidden = grad_y + grad_from_two
    grad_attn = grad_hidden.astype(jnp.bfloat16)
    g_out = weight_grad(context, grad_attn)
    g_bout = column_sums(grad_attn)
    grad_context = project_back(grad_attn, w_out).astype(jnp.bfloat16)
    grad_context_whole = lax.all_to_all(
        grad_context, "seq", split_axis=2, concat_axis=1, tiled=True
    )
    grad_q_whole, grad_k_whole, grad_v_whole = lax.map(
        attend_back, (query_whole, key_whole, value_whole, grad_context_whole, log_totals, lengths)
    )
    grad_queries, grad_keys, grad_values = (
        lax.all_to_all(grad_q_whole, "seq", split_axis=1, concat_axis=2, tiled=True),
        lax.all_to_all(grad_k_whole, "seq", split_axis=1, concat_axis=2, tiled=True),
        lax.all_to_all(grad_v_whole, "seq", split_axis=1, concat_axis=2, tiled=True),
    )
    g_query = weight_grad(normed_one, grad_queries)
    g_bquery = column_sums(grad_queries)
    g_key = weight_grad(normed_one, grad_keys)
    g_value = weight_grad(normed_one, grad_values)
    g_bvalue = column_sums(grad_values)
    grad_normed_one = (
        project_back(grad_queries, w_query)
        + project_back(grad_keys, w_key)
        + project_back(grad_values, w_value)
    )
    grad_from_one, g_gain_one, g_shift_one = norm_backward(
        grad_normed_one, scaled_one, rstd_one, gain_one
    )
    grad_patches = (grad_hidden + grad_from_one).astype(jnp.bfloat16)
    (
        g_gain_one,
        g_shift_one,
        g_query,
        g_bquery,
        g_key,
        g_value,
        g_bvalue,
        g_out,
        g_bout,
        g_gain_two,
        g_shift_two,
        g_up,
        g_bup,
        g_down,
        g_bdown,
    ) = lax.psum(
        (
            g_gain_one,
            g_shift_one,
            g_query,
            g_bquery,
            g_key,
            g_value,
            g_bvalue,
            g_out,
            g_bout,
            g_gain_two,
            g_shift_two,
            g_up,
            g_bup,
            g_down,
            g_bdown,
        ),
        ("dp", "seq"),
    )
    return (
        output,
        grad_patches,
        g_gain_one,
        g_shift_one,
        g_query,
        g_bquery,
        g_key,
        g_value,
        g_bvalue,
        g_out,
        g_bout,
        g_gain_two,
        g_shift_two,
        g_up,
        g_bup,
        g_down,
        g_bdown,
    )


def solution(mesh):
    return jax.shard_map(
        local,
        mesh=mesh,
        in_specs=(
            P("dp", "seq", None),
            P("dp"),
            P(),
            P(),
            P(),
            P(),
            P(),
            P(),
            P(),
            P(),
            P(),
            P(),
            P(),
            P(),
            P(),
            P(),
            P(),
            P("dp", "seq", None),
        ),
        out_specs=(
            P("dp", "seq", None),
            P("dp", "seq", None),
            P(),
            P(),
            P(),
            P(),
            P(),
            P(),
            P(),
            P(),
            P(),
            P(),
            P(),
            P(),
            P(),
            P(),
            P(),
        ),
        check_vma=False,
    )
```

profile of v0, /device:TPU:0, one launch (start us, length us, event | category | flops | bytes accessed | tf_op | source)
XLA Modules:
  0.0 909.4 jit_solution(8345375993950918164)
XLA Ops:
  11.3 2.9 add_convert_fusion.4
  14.2 5.1 copy.101
  19.4 5.1 all-to-all-start
  24.5 4.2 add_convert_fusion.3
  28.7 5.1 copy.104
  33.9 4.9 all-to-all-start.1
  38.8 7.2 copy.136
  46.0 2.8 copy.103
  48.8 3.8 copy.110
  52.6 4.2 convolution_convert_fusion.1
  56.8 5.1 copy.107
  62.0 5.5 all-to-all-start.2
  67.4 7.2 copy.137
  74.6 2.8 copy.106
  77.4 3.8 copy.111
  81.3 7.2 copy.138
  88.5 2.8 copy.109
  91.3 3.8 copy.112
  96.6 45.2 %while.26 = (s32[]{:T(128)}, bf16[4,544,384]{1,2,0:T(8,128)(2,1)}, f32[4,6,544]{2,1,0:T(8,128)}, bf16[4,544,384]{1,2,0:T(8,128)(2,1)}, s32[4]{0:T(128)S(1)}, /*i...) while((s32[]{:T(128)}, bf16[4,544,384]{1,2,0:T(8,128)(2,1)}, ...), condition=%wide.region_5.6_spmd, body=%wide.region_2.5_spmd.sunk | while | flops 476071264 | bytes 26508796 | solution.py:140
  104.1 2.3 fusion.122
  141.8 4.7 copy.113
  146.5 6.4 all_to_all.144
  156.7 11.9 %fusion.47 = (u8[272,3072]{1,0:T(8,128)(4,1)S(1)}, u8[272,3072]{1,0:T(8,128)(4,1)S(1)}, f32[4,272,3072]{2,1,0:T(8,128)S(1)}) fusion(f32[3072]{0:T(1024)S(1)} %copy-done.30, bf16[768,3072]{1,0:T(8,128)(2,1)} %param.35, f32[4,272,768]{2,1,0:T(8,128)S(1)} %get-tuple-element.238, f32[768]{0:T(1024)S(1)} %copy-done.44, f32[768]{0:T(1024)S(1)} %copy-done.32, ...), kind=kOutput, calls=%fused_computation.101 | convolution fusion | flops 5183127552 | bytes 23128576 | tf_op jit(solution)/shard_map/dot_general | solution.py:15
  168.6 32.4 %multiply_convert_fusion.1 = (bf16[4,272,3072]{2,1,0:T(8,128)(2,1)}, f32[4,272,3072]{2,1,0:T(8,128)}) fusion(f32[4,272,3072]{2,1,0:T(8,128)S(1)} %get-tuple-element.239, f32[3072]{0:T(1024)S(1)} %copy-done.30, u8[272,3072]{1,0:T(8,128)(4,1)S(1)} %get-tuple-element.166, u8[272,3072]{1,0:T(8,128)(4,1)S(1)} %get-tuple-element.165), kind=kLoop, calls=%fused_computation.46 | loop fusion | flops 237305856 | bytes 35106816 | tf_op jit(solution)/shard_map/convert_element_type | solution.py:145
  201.0 19.9 %convert_reduce_fusion = (f32[3072]{0:T(1024)}, bf16[4,272,3072]{2,1,0:T(8,128)(2,1)}) fusion(f32[4,272,3072]{2,1,0:T(8,128)} %get-tuple-element.227, bf16[4,272,768]{2,1,0:T(8,128)(2,1)} %param.39, bf16[3072,768]{1,0:T(8,128)(2,1)} %param.37, f32[4,272,3072]{2,1,0:T(8,128)} %copy-done.9, f32[3072]{0:T(1024)S(1)} %copy-done.30), kind=kOutput, calls=%fused_computation.44 | convolution fusion | flops 5190644736 | bytes 39837696 | tf_op jit(solution)/shard_map/stf,df->std/dot_general | solution.py:19
  220.9 10.6 %multiply_reduce_fusion.1 = (f32[768]{0:T(1024)}, f32[4,272]{1,0:T(4,128)S(1)}, f32[4,272]{1,0:T(4,128)S(1)}, f32[768]{0:T(1024)}, f32[4,272,768]{2,1,0:T(8,128)S(1)}) fusion(f32[4,272,768]{2,1,0:T(8,128)S(1)} %copy-done.6, f32[4,272]{1,0:T(4,128)S(1)} %add_rsqrt_fusion, f32[4,272]{1,0:T(4,128)S(1)} %broadcast_multiply_fusion.4, f32[768]{0:T(1024)S(1)} %copy-done.32, ...), kind=kOutput, calls=%fused_computation.89 | convolution fusion | flops 5141344256 | bytes 18114560 | tf_op jit(solution)/shard_map/stf,df->std/dot_general | solution.py:19
  235.6 2.7 convolution_convert_fusion
  238.3 3.9 copy.116
  242.3 6.9 all_to_all.145
  249.2 7.0 copy.139
  261.9 104.6 %while.27 = (s32[]{:T(128)}, bf16[4,544,384]{1,2,0:T(8,128)(2,1)}, bf16[4,544,384]{1,2,0:T(8,128)(2,1)}, bf16[4,544,384]{1,2,0:T(8,128)(2,1)}, bf16[4,544,384]{1...) while((s32[]{:T(128)}, bf16[4,544,384]{1,2,0:T(8,128)(2,1)}, ...), condition=%wide.region_12.13_spmd, body=%wide.region_10.12_spmd.sunk | while | flops 1164070272 | bytes 89513552 | solution.py:167
  264.0 4.7 fusion.133
  273.1 5.9 multiply_reduce_fusion.7
  279.1 2.6 multiply_convert_fusion.3
  290.2 4.7 fusion.133
  299.3 5.9 multiply_reduce_fusion.7
  305.2 2.6 multiply_convert_fusion.3
  316.4 4.7 fusion.133
  325.4 5.9 multiply_reduce_fusion.7
  331.4 2.6 multiply_convert_fusion.3
  342.5 4.7 fusion.133
  351.6 5.9 multiply_reduce_fusion.7
  357.6 2.6 multiply_convert_fusion.3
  366.5 4.8 copy.129
  371.3 4.7 all-to-all-start.7
  376.0 5.2 convolution_bitcast_fusion.2
  381.3 12.3 %convolution_bitcast_fusion.1 = f32[768,3072]{1,0:T(8,128)} fusion(bf16[4,272,3072]{2,1,0:T(8,128)(2,1)} %get-tuple-element.243, f32[4,272,768]{2,1,0:T(8,128)S(1)} %copy-done.7, f32[768]{0:T(1024)S(1)} %copy-done.45, f32[768]{0:T(1024)S(1)} %copy-done.33, f32[4,272]{1,0:T(4,128)S(1)} %add_rsqrt_fusion, f32[4,272]{1,0:T(4,128)S(1)} %broadcast_multiply_fusion.4), kind=kOutput, calls=%fused_computation.60 | convolution fusion | flops 5138006016 | bytes 19479040 | tf_op jit(solution)/shard_map/std,stf->df/dot_general | solution.py:23
  393.6 3.0 copy.123
  396.6 4.7 all-to-all-start.5
  404.3 4.7 copy.126
  409.0 4.6 all-to-all-start.6
  420.4 3.6 convolution_bitcast_fusion.5
  423.9 3.6 convolution_bitcast_fusion.4
  427.5 3.6 convolution_bitcast_fusion.3
  431.1 9.1 %convolution_bitcast_fusion = f32[3072,768]{1,0:T(8,128)} fusion(bf16[4,272,3072]{2,1,0:T(8,128)(2,1)S(1)} %bitcast.225, bf16[4,272,768]{2,1,0:T(8,128)(2,1)S(1)} %copy-done.23), kind=kOutput, calls=%fused_computation.59 | convolution fusion | flops 5133828096 | bytes 17793024 | tf_op jit(solution)/shard_map/std,stf->df/dot_general | solution.py:23
  442.3 3.4 fusion.55
  447.7 3.8 fusion.43
  451.6 45.7 %all-reduce = (f32[768]{0:T(1024)}, f32[768]{0:T(1024)}, f32[768]{0:T(1024)}, f32[768]{0:T(1024)}, f32[768]{0:T(1024)}, /*index=5*/f32[768]{0:T(1024)}, f32[768]{0:T(1024)}, f32[3072]{0:T(1024)}, f32[768]{0:T(1024)}) all-reduce(f32[768]{0:T(1024)S(1)} %get-tuple-element.169, ...), channel_id=1, replica_groups=mesh['dp'=16,'seq'=2] {'dp','seq'}, use_global_device_ids=true, to_apply=%region_16.17 | all-reduce | flops 9216 | bytes 73728 | tf_op jit(solution)/shard_map/psum | solution.py:205
  497.4 5.2 fusion.42
  502.6 10.0 %add_convert_fusion.1 = bf16[4,272,768]{2,1,0:T(8,128)(2,1)} fusion(f32[4,272,768]{2,1,0:T(8,128)S(1)} %copy-done.8, bf16[4,272,3072]{2,1,0:T(8,128)(2,1)} %get-tuple-element.226, bf16[3072,768]{1,0:T(8,128)(2,1)} %param.37, f32[768]{0:T(1024)S(1)} %copy-done.48), kind=kOutput, calls=%fused_computation.95 | convolution fusion | flops 5136334848 | bytes 16419840 | tf_op jit(solution)/shard_map/dot_general | solution.py:15
  512.6 366.8 %all-reduce.4.cloned.1.call-done = (f32[768,768]{1,0:T(8,128)}, f32[768,768]{1,0:T(8,128)}, f32[768,768]{1,0:T(8,128)}, f32[768,768]{1,0:T(8,128)}, f32[768,3072]{1,0:T(8,128)}, /*index=5*/f32[3072,768]{1,0:T(8,128)}) async-done(((f32[768,768]{1,0:T(8,128)}, f32[768,768]{1,0:T(8,128)}, f32[768,768]{1,0:T(8,128)}, f32[768,768]{1,0:T(8,128)}, f32[768,3072]{1,0:T(8,128)}, /*index=5*/f32[3072,768]{1,0:T(8,128)}), ...) | async-done | bytes 28311568 | tf_op jit(solution)/shard_map/psum | solution.py:205
  879.4 3.4 copy.181
  889.2 9.3 %copy.185 = f32[768,3072]{1,0:T(8,128)} copy(f32[768,3072]{1,0:T(8,128)} %get-tuple-element.436) | data formatting | bytes 18874368
  898.5 3.7 copy.186
  (263 shorter events, 133.5 us)
Async XLA Ops:
  7.2 4.1 copy-start
  7.2 4.1 copy-start.2
  7.2 4.0 copy-start.41
  7.2 4.0 copy-start.46
  7.2 4.0 copy-start.34
  9.2 43.5 %copy-start.24 = (f32[4,272]{1,0:T(4,128)}, f32[4,272]{1,0:T(4,128)S(1)}, u32[]{:S(2)}) copy-start(f32[4,272]{1,0:T(4,128)S(1)} %broadcast_multiply_fusion.5) | copy-start | bytes 13060
  11.3 41.3 %copy-start.26 = (f32[4,272]{1,0:T(4,128)}, f32[4,272]{1,0:T(4,128)S(1)}, u32[]{:S(2)}) copy-start(f32[4,272]{1,0:T(4,128)S(1)} %add_rsqrt_fusion.1) | copy-start | bytes 13060
  19.4 5.1 copy-start.42
  19.4 14.5 %all-to-all-start = ((bf16[4,272,768]{1,0,2:T(4,128)(2,1)}), bf16[4,272,768]{1,0,2:T(4,128)(2,1)}, u32[]{:S(2)}, u32[]{:S(2)}) async-start(bf16[4,272,768]{1,0,2:T(4,128)(2,1)} %copy.101), calls=%async_computation | async-start | bytes 4718592 | tf_op jit(solution)/shard_map/all_to_all | solution.py:138
  33.9 28.1 %all-to-all-start.1 = ((bf16[4,272,768]{1,0,2:T(4,128)(2,1)}), bf16[4,272,768]{1,0,2:T(4,128)(2,1)}, u32[]{:S(2)}, u32[]{:S(2)}) async-start(bf16[4,272,768]{1,0,2:T(4,128)(2,1)} %copy.104), calls=%async_computation.1 | async-start | bytes 4718592 | tf_op jit(solution)/shard_map/all_to_all | solution.py:136
  62.0 19.3 %all-to-all-start.2 = ((bf16[4,272,768]{1,0,2:T(4,128)(2,1)}), bf16[4,272,768]{1,0,2:T(4,128)(2,1)}, u32[]{:S(2)}, u32[]{:S(2)}) async-start(bf16[4,272,768]{1,0,2:T(4,128)(2,1)} %copy.107), calls=%async_computation.2 | async-start | bytes 4718592 | tf_op jit(solution)/shard_map/all_to_all | solution.py:137
  91.3 5.3 copy-start.49
  153.3 2.6 copy-start.15
  155.9 12.7 %copy-start.5 = (f32[4,272,768]{2,1,0:T(8,128)}, f32[4,272,768]{2,1,0:T(8,128)S(1)}, u32[]{:S(2)}) copy-start(f32[4,272,768]{2,1,0:T(8,128)S(1)} %get-tuple-element.238) | copy-start | bytes 10027012
  168.6 32.4 %copy-start.9 = (f32[4,272,3072]{2,1,0:T(8,128)}, f32[4,272,3072]{2,1,0:T(8,128)S(1)}, u32[]{:S(2)}) copy-start(f32[4,272,3072]{2,1,0:T(8,128)S(1)} %get-tuple-element.239) | copy-start | bytes 40108036
  201.0 19.9 %copy-start.6 = (f32[4,272,768]{2,1,0:T(8,128)S(1)}, f32[4,272,768]{2,1,0:T(8,128)}, u32[]{:S(2)}) copy-start(f32[4,272,768]{2,1,0:T(8,128)} %copy-done.5) | copy-start | bytes 10027012
  220.9 10.6 %copy-start.22 = (bf16[4,272,768]{2,1,0:T(8,128)(2,1)S(1)}, bf16[4,272,768]{2,1,0:T(8,128)(2,1)}, u32[]{:S(2)}) copy-start(bf16[4,272,768]{2,1,0:T(8,128)(2,1)} %param.39) | copy-start | bytes 5013508
  231.5 4.1 copy-start.39
  233.8 1.8 copy-start.10
  257.6 4.3 copy-start.50
  273.1 6.0 slice-start
  273.1 6.0 slice-start.1
  299.2 6.0 slice-start
  299.3 6.0 slice-start.1
  325.4 6.0 slice-start
  325.4 6.0 slice-start.1
  351.6 6.0 slice-start
  351.6 6.0 slice-start.1
  366.5 9.5 %copy-start.16 = (bf16[4,2,34,8,384]{4,3,1,2,0:T(8,128)(2,1)S(1)}, bf16[4,2,34,8,384]{4,3,1,2,0:T(8,128)(2,1)}, u32[]{:S(2)}) copy-start(bf16[4,2,34,8,384]{4,3,1,2,0:T(8,128)(2,1)} %copy-done.15) | copy-start | bytes 5013508
  371.3 25.3 %all-to-all-start.7 = ((bf16[4,544,384]{2,0,1:T(4,128)(2,1)}), bf16[4,544,384]{2,0,1:T(4,128)(2,1)}, u32[]{:S(2)}, u32[]{:S(2)}) async-start(bf16[4,544,384]{2,0,1:T(4,128)(2,1)} %copy.129), calls=%async_computation.7 | async-start | bytes 3342336 | tf_op jit(solution)/shard_map/all_to_all | solution.py:173
  376.0 5.3 copy-start.7
  376.0 5.3 copy-start.33
  376.0 5.3 copy-start.45
  381.3 12.3 %copy-start.11 = (bf16[4,544,384]{1,2,0:T(8,128)(2,1)S(1)}, bf16[4,544,384]{1,2,0:T(8,128)(2,1)}, u32[]{:S(2)}) copy-start(bf16[4,544,384]{1,2,0:T(8,128)(2,1)} %get-tuple-element.111) | copy-start | bytes 5013508
  396.6 12.4 %all-to-all-start.5 = ((bf16[4,544,384]{2,0,1:T(4,128)(2,1)}), bf16[4,544,384]{2,0,1:T(4,128)(2,1)}, u32[]{:S(2)}, u32[]{:S(2)}) async-start(bf16[4,544,384]{2,0,1:T(4,128)(2,1)} %copy.123), calls=%async_computation.5 | async-start | bytes 3342336 | tf_op jit(solution)/shard_map/all_to_all | solution.py:171
  409.0 8.9 all-to-all-start.6
  413.6 465.8 %all-reduce.4.cloned.1.call-start = ((), (), s32[]{:S(2)}) async-start(), calls=%async_computation.8 | async-start | bytes 56623104 | tf_op jit(solution)/shard_map/psum | solution.py:205
  417.8 2.0 copy-start.25
  417.8 2.1 copy-start.27
  417.8 2.1 copy-start.35
  417.9 2.1 copy-start.47
  417.9 2.1 copy-start.3
  417.9 2.5 copy-start.19
  419.9 4.0 copy-start.20
  423.9 3.6 copy-start.17
  423.9 7.2 slice-start.5
  427.5 3.6 slice-start.6
  427.5 3.6 copy-start.23
  442.3 3.5 copy-start.21
  442.3 3.5 copy-start.40
  445.8 1.9 copy-start.18
  447.7 3.9 copy-start.28
  447.7 3.9 copy-start.29
  447.7 3.9 copy-start.31
  447.7 3.9 copy-start.36
  447.7 3.9 copy-start.37
  497.4 5.2 copy-start.8
  497.4 5.2 copy-start.48
  879.4 3.4 copy-start.14
  882.8 2.5 copy-start.13
  885.3 2.5 copy-start.12
  887.8 10.7 %slice-start.2 = ((s8[9437184]{0:T(1024)(128)(4,1)}), s8[4194304]{0:T(1024)(128)(4,1)S(1)}, s32[]{:S(2)}) async-start(s8[9437184]{0:T(1024)(128)(4,1)} %bitcast.211), calls=%async_computation.11 | async-start | bytes 8388608
  889.2 9.3 %slice-start.3 = ((s8[9437184]{0:T(1024)(128)(4,1)}), s8[4194304]{0:T(1024)(128)(4,1)S(1)}, s32[]{:S(2)}) async-start(s8[9437184]{0:T(1024)(128)(4,1)} %bitcast.211), calls=%async_computation.12 | async-start | bytes 8388608
  889.2 9.3 %slice-start.4 = ((s8[9437184]{0:T(1024)(128)(4,1)}), s8[1048576]{0:T(1024)(128)(4,1)S(1)}, s32[]{:S(2)}) async-start(s8[9437184]{0:T(1024)(128)(4,1)} %bitcast.211), calls=%async_computation.13 | async-start | bytes 2097152
  (7 other events, 7.6 us)
Sparse Core Ops, SparseCore 0:
  440.4 438.9 all-reduce.3
where the time goes:
time: 919 us; the launch traced here: 909 us
  waiting for transfers between devices  367 us (40%)
  matrix products  192 us (21%)
  local copies, waits for them, and re-layouts  175 us (19%)
  other arithmetic  72.5 us (8%)
  blocking collectives  59.1 us (6%)
  starting transfers between devices  29.5 us (3%)
  between operations  14.9 us (2%)
    psum x1, waiting for transfers between devices, local(): lax.psum((g_gain_one, g_shift_one, g_query, g_bquery, g_key, g_value, g_b...  367 us
    psum x1, blocking collectives, local(): lax.psum((g_gain_one, g_shift_one, g_query, g_bquery, g_key, g_value, g_b...  45.7 us
    dot_general x6, matrix products, project_back(): jnp.einsum('stf,df->std', grad_rows, weight, preferred_element_type=jnp.f...  42 us
    dot_general x6, matrix products, weight_grad(): jnp.einsum('std,stf->df', left_rows, grad_rows, preferred_element_type=jn...  37.4 us
    dot_general x6, matrix products, project(): return jnp.dot(left_rows, weight, preferred_element_type=jnp.float32)  34.9 us
    convert_element_type x1, other arithmetic, local(): active = exact_gelu(upper_pre).astype(jnp.bfloat16)  32.4 us
    dynamic_slice x36, local copies, waits for them, and re-layouts, local(): lax.map(attend, (query_whole, key_whole, value_whole, lengths))  32.2 us
    unnamed x118, local copies, waits for them, and re-layouts  28 us
  transfers between devices with their start and end apart: 7, of which 1 were waited for; matrix products, arithmetic and copies ran while one was open for 11% of the time, Pallas kernels for 0%

commit v1 on v0

--- a/solution.py
+++ b/solution.py
@@ -5,6 +5,10 @@
 
 HEAD_DIM = 64
 epsilon = 1e-06
+
+
+def pages_point(field_in, row_axis, axis_tag):
+    return lax.psum(lax.psum(field_in, axis_name=row_axis), axis_name=axis_tag)
 
 
 def exact_gelu(values):
@@ -202,7 +206,7 @@
         g_bup,
         g_down,
         g_bdown,
-    ) = lax.psum(
+    ) = pages_point(
         (
             g_gain_one,
             g_shift_one,
@@ -220,7 +224,8 @@
             g_down,
             g_bdown,
         ),
-        ("dp", "seq"),
+        "seq",
+        "dp",
     )
     return (
         output,

time: 919 us -> 1340 us (1.46)
  waiting for transfers between devices: 367 us -> 743 us
  blocking collectives: 59.1 us -> 99.5 us
    psum x1 -> x2, waiting for transfers between devices: 367 us -> 743 us  [pages_point(): return lax.psum(lax.psum(field_in, axis_name=row_axis), axis_name=axis_tag)]
    psum x1 -> x2, blocking collectives: 45.7 us -> 86.2 us  [pages_point(): return lax.psum(lax.psum(field_in, axis_name=row_axis), axis_name=axis_tag)]
  transfers between devices with their start and end apart: 7 -> 8, of which waited for: 1 -> 2; matrix products, arithmetic and copies ran while one was open for 11% -> 8% of each run, Pallas kernels for 0% -> 0%
where the time goes in v1:
time: 1340 us; the launch traced here: 1330 us
  waiting for transfers between devices  743 us (55%)
  matrix products  192 us (14%)
  local copies, waits for them, and re-layouts  174 us (13%)
  blocking collectives  99.5 us (7%)
  other arithmetic  71.9 us (5%)
  starting transfers between devices  29.5 us (2%)
  between operations  14.9 us (1%)
    psum x2, waiting for transfers between devices, pages_point(): return lax.psum(lax.psum(field_in, axis_name=row_axis), axis_name=axis_tag)  743 us
    psum x2, blocking collectives, pages_point(): return lax.psum(lax.psum(field_in, axis_name=row_axis), axis_name=axis_tag)  86.2 us
    dot_general x6, matrix products, project_back(): jnp.einsum('stf,df->std', grad_rows, weight, preferred_element_type=jnp.f...  42.1 us
    dot_general x6, matrix products, weight_grad(): jnp.einsum('std,stf->df', left_rows, grad_rows, preferred_element_type=jn...  37.4 us
    dot_general x6, matrix products, project(): return jnp.dot(left_rows, weight, preferred_element_type=jnp.float32)  34.7 us
    convert_element_type x1, other arithmetic, local(): active = exact_gelu(upper_pre).astype(jnp.bfloat16)  32.4 us
    dynamic_slice x36, local copies, waits for them, and re-layouts, local(): lax.map(attend, (query_whole, key_whole, value_whole, lengths))  32.2 us
    unnamed x118, local copies, waits for them, and re-layouts  27.9 us
  transfers between devices with their start and end apart: 8, of which 2 were waited for; matrix products, arithmetic and copies ran while one was open for 8% of the time, Pallas kernels for 0%

profile of v1, /device:TPU:0, one launch (start us, length us, event | category | flops | bytes accessed | tf_op | source)
XLA Modules:
  0.0 1325.9 jit_solution(5285887293343845159)
XLA Ops:
  11.3 2.9 add_convert_fusion.4
  14.2 5.1 copy.101
  19.4 5.1 all-to-all-start
  24.5 4.2 add_convert_fusion.3
  28.7 5.1 copy.104
  33.8 4.9 all-to-all-start.1
  38.8 7.2 copy.136
  46.0 2.8 copy.103
  48.8 3.8 copy.110
  52.6 4.2 convolution_convert_fusion.1
  56.8 5.1 copy.107
  62.0 5.5 all-to-all-start.2
  67.4 7.2 copy.137
  74.6 2.8 copy.106
  77.4 3.8 copy.111
  81.3 7.2 copy.138
  88.4 2.8 copy.109
  91.3 3.8 copy.112
  96.5 45.2 %while.26 = (s32[]{:T(128)}, bf16[4,544,384]{1,2,0:T(8,128)(2,1)}, f32[4,6,544]{2,1,0:T(8,128)}, bf16[4,544,384]{1,2,0:T(8,128)(2,1)}, s32[4]{0:T(128)S(1)}, /*i...) while((s32[]{:T(128)}, bf16[4,544,384]{1,2,0:T(8,128)(2,1)}, ...), condition=%wide.region_5.6_spmd, body=%wide.region_2.5_spmd.sunk | while | flops 476071264 | bytes 26508796 | solution.py:144
  141.8 4.7 copy.113
  146.5 6.4 all_to_all.144
  156.7 11.9 fusion.47
  168.6 32.4 %multiply_convert_fusion.1 = (bf16[4,272,3072]{2,1,0:T(8,128)(2,1)}, f32[4,272,3072]{2,1,0:T(8,128)}) fusion(f32[4,272,3072]{2,1,0:T(8,128)S(1)} %get-tuple-element.254, f32[3072]{0:T(1024)S(1)} %copy-done.30, u8[272,3072]{1,0:T(8,128)(4,1)S(1)} %get-tuple-element.166, u8[272,3072]{1,0:T(8,128)(4,1)S(1)} %get-tuple-element.165), kind=kLoop, calls=%fused_computation.46 | loop fusion | flops 237305856 | bytes 35106816 | tf_op jit(solution)/shard_map/convert_element_type | solution.py:149
  200.9 19.9 %convert_reduce_fusion = (f32[3072]{0:T(1024)}, bf16[4,272,3072]{2,1,0:T(8,128)(2,1)}) fusion(f32[4,272,3072]{2,1,0:T(8,128)} %get-tuple-element.242, bf16[4,272,768]{2,1,0:T(8,128)(2,1)} %param.39, bf16[3072,768]{1,0:T(8,128)(2,1)} %param.37, f32[4,272,3072]{2,1,0:T(8,128)} %copy-done.9, f32[3072]{0:T(1024)S(1)} %copy-done.30), kind=kOutput, calls=%fused_computation.44 | convolution fusion | flops 5190644736 | bytes 39837696 | tf_op jit(solution)/shard_map/stf,df->std/dot_general | solution.py:23
  220.9 10.6 multiply_reduce_fusion.1
  235.5 2.7 convolution_convert_fusion
  238.2 3.9 copy.116
  242.1 6.9 all_to_all.145
  249.0 7.0 copy.139
  261.8 105.1 %while.27 = (s32[]{:T(128)}, bf16[4,544,384]{1,2,0:T(8,128)(2,1)}, bf16[4,544,384]{1,2,0:T(8,128)(2,1)}, bf16[4,544,384]{1,2,0:T(8,128)(2,1)}, bf16[4,544,384]{1...) while((s32[]{:T(128)}, bf16[4,544,384]{1,2,0:T(8,128)(2,1)}, ...), condition=%wide.region_12.13_spmd, body=%wide.region_10.12_spmd.sunk | while | flops 1164070272 | bytes 89513552 | solution.py:171
  263.9 4.7 fusion.133
  273.0 6.1 multiply_reduce_fusion.7
  279.1 2.6 multiply_convert_fusion.3
  290.2 4.7 fusion.133
  299.3 6.1 multiply_reduce_fusion.7
  305.4 2.6 multiply_convert_fusion.3
  316.4 4.7 fusion.133
  325.5 6.1 multiply_reduce_fusion.7
  342.7 4.7 fusion.133
  351.8 6.1 multiply_reduce_fusion.7
  357.9 2.6 multiply_convert_fusion.3
  366.9 4.8 copy.129
  371.7 4.7 all-to-all-start.7
  376.4 5.2 convolution_bitcast_fusion.2
  381.6 12.3 convolution_bitcast_fusion.1
  394.0 3.0 copy.123
  396.9 4.7 all-to-all-start.5
  404.6 4.7 copy.126
  409.3 4.7 all-to-all-start.6
  420.7 3.6 convolution_bitcast_fusion.5
  424.3 3.6 convolution_bitcast_fusion.4
  427.9 3.6 convolution_bitcast_fusion.3
  431.5 9.1 convolution_bitcast_fusion
  440.6 94.4 %all-reduce.9.cloned.1.call-done = (f32[768,768]{1,0:T(8,128)}, f32[768,768]{1,0:T(8,128)}, f32[768,768]{1,0:T(8,128)}, f32[768,768]{1,0:T(8,128)}, f32[768,3072]{1,0:T(8,128)}, /*index=5*/f32[3072,768]{1,0:T(8,128)}) async-done(((f32[768,768]{1,0:T(8,128)}, f32[768,768]{1,0:T(8,128)}, f32[768,768]{1,0:T(8,128)}, f32[768,768]{1,0:T(8,128)}, f32[768,3072]{1,0:T(8,128)}, /*index=5*/f32[3072,768]{1,0:T(8,128)}), ...) | async-done | bytes 28311568 | tf_op jit(solution)/shard_map/psum | solution.py:11
  537.2 3.4 fusion.55
  542.6 3.9 fusion.43
  546.5 3.6 all-reduce.2
  550.2 82.6 %all-reduce = (f32[768]{0:T(1024)}, f32[768]{0:T(1024)}, f32[768]{0:T(1024)}, f32[768]{0:T(1024)}, f32[768]{0:T(1024)}, /*index=5*/f32[768]{0:T(1024)}, f32[768]{0:T(1024)}, f32[3072]{0:T(1024)}, f32[768]{0:T(1024)}) all-reduce(f32[768]{0:T(1024)S(1)} %get-tuple-element.224, ...), channel_id=1, replica_groups=mesh['dp'=16,'seq'=2] {'dp'}, use_global_device_ids=true, to_apply=%region_17.18 | all-reduce | flops 9216 | bytes 73728 | tf_op jit(solution)/shard_map/psum | solution.py:11
  632.7 4.7 fusion.42
  637.4 9.8 add_convert_fusion.1
  647.2 648.6 %all-reduce.7.cloned.1.call-done = (f32[768,768]{1,0:T(8,128)}, f32[768,768]{1,0:T(8,128)}, f32[768,768]{1,0:T(8,128)}, f32[768,768]{1,0:T(8,128)}, f32[768,3072]{1,0:T(8,128)}, /*index=5*/f32[3072,768]{1,0:T(8,128)}) async-done(((f32[768,768]{1,0:T(8,128)}, f32[768,768]{1,0:T(8,128)}, f32[768,768]{1,0:T(8,128)}, f32[768,768]{1,0:T(8,128)}, f32[768,3072]{1,0:T(8,128)}, /*index=5*/f32[3072,768]{1,0:T(8,128)}), ...) | async-done | bytes 28311568 | tf_op jit(solution)/shard_map/psum | solution.py:11
  1295.9 3.4 copy.187
  1305.7 9.3 copy.191
  1315.0 3.7 copy.192
  (267 shorter events, 138.3 us)
Async XLA Ops:
  7.2 4.1 copy-start
  7.2 4.1 copy-start.2
  7.2 4.0 copy-start.41
  7.2 4.0 copy-start.46
  7.2 4.0 copy-start.34
  9.2 43.5 %copy-start.24 = (f32[4,272]{1,0:T(4,128)}, f32[4,272]{1,0:T(4,128)S(1)}, u32[]{:S(2)}) copy-start(f32[4,272]{1,0:T(4,128)S(1)} %broadcast_multiply_fusion.5) | copy-start | bytes 13060
  11.3 41.3 %copy-start.26 = (f32[4,272]{1,0:T(4,128)}, f32[4,272]{1,0:T(4,128)S(1)}, u32[]{:S(2)}) copy-start(f32[4,272]{1,0:T(4,128)S(1)} %add_rsqrt_fusion.1) | copy-start | bytes 13060
  19.4 5.1 copy-start.42
  19.4 14.5 %all-to-all-start = ((bf16[4,272,768]{1,0,2:T(4,128)(2,1)}), bf16[4,272,768]{1,0,2:T(4,128)(2,1)}, u32[]{:S(2)}, u32[]{:S(2)}) async-start(bf16[4,272,768]{1,0,2:T(4,128)(2,1)} %copy.101), calls=%async_computation | async-start | bytes 4718592 | tf_op jit(solution)/shard_map/all_to_all | solution.py:142
  33.8 28.1 %all-to-all-start.1 = ((bf16[4,272,768]{1,0,2:T(4,128)(2,1)}), bf16[4,272,768]{1,0,2:T(4,128)(2,1)}, u32[]{:S(2)}, u32[]{:S(2)}) async-start(bf16[4,272,768]{1,0,2:T(4,128)(2,1)} %copy.104), calls=%async_computation.1 | async-start | bytes 4718592 | tf_op jit(solution)/shard_map/all_to_all | solution.py:140
  62.0 19.3 %all-to-all-start.2 = ((bf16[4,272,768]{1,0,2:T(4,128)(2,1)}), bf16[4,272,768]{1,0,2:T(4,128)(2,1)}, u32[]{:S(2)}, u32[]{:S(2)}) async-start(bf16[4,272,768]{1,0,2:T(4,128)(2,1)} %copy.107), calls=%async_computation.2 | async-start | bytes 4718592 | tf_op jit(solution)/shard_map/all_to_all | solution.py:141
  91.3 5.3 copy-start.49
  153.3 2.6 copy-start.15
  155.8 12.7 copy-start.5
  168.5 32.4 %copy-start.9 = (f32[4,272,3072]{2,1,0:T(8,128)}, f32[4,272,3072]{2,1,0:T(8,128)S(1)}, u32[]{:S(2)}) copy-start(f32[4,272,3072]{2,1,0:T(8,128)S(1)} %get-tuple-element.254) | copy-start | bytes 40108036
  200.9 19.9 %copy-start.6 = (f32[4,272,768]{2,1,0:T(8,128)S(1)}, f32[4,272,768]{2,1,0:T(8,128)}, u32[]{:S(2)}) copy-start(f32[4,272,768]{2,1,0:T(8,128)} %copy-done.5) | copy-start | bytes 10027012
  220.9 10.6 copy-start.22
  231.5 4.0 copy-start.39
  257.4 4.3 copy-start.50
  273.0 6.1 slice-start
  273.0 6.1 slice-start.1
  299.2 6.1 slice-start
  299.3 6.1 slice-start.1
  325.5 6.1 slice-start
  325.5 6.1 slice-start.1
  351.8 6.1 slice-start
  351.8 6.1 slice-start.1
  366.9 9.5 copy-start.16
  371.7 25.3 %all-to-all-start.7 = ((bf16[4,544,384]{2,0,1:T(4,128)(2,1)}), bf16[4,544,384]{2,0,1:T(4,128)(2,1)}, u32[]{:S(2)}, u32[]{:S(2)}) async-start(bf16[4,544,384]{2,0,1:T(4,128)(2,1)} %copy.129), calls=%async_computation.7 | async-start | bytes 3342336 | tf_op jit(solution)/shard_map/all_to_all | solution.py:177
  376.3 5.3 copy-start.7
  376.3 5.3 copy-start.33
  376.4 5.3 copy-start.45
  381.6 12.3 copy-start.11
  396.9 12.3 all-to-all-start.5
  409.3 8.9 all-to-all-start.6
  414.0 121.1 %all-reduce.9.cloned.1.call-start = ((), (), s32[]{:S(2)}) async-start(), calls=%async_computation.9 | async-start | bytes 56623104 | tf_op jit(solution)/shard_map/psum | solution.py:11
  418.2 2.0 copy-start.25
  418.2 2.1 copy-start.27
  418.2 2.1 copy-start.35
  418.2 2.1 copy-start.47
  418.2 2.1 copy-start.3
  418.2 2.5 copy-start.19
  420.2 4.0 copy-start.20
  424.3 3.6 copy-start.17
  424.3 7.1 slice-start.5
  427.9 3.6 slice-start.6
  427.9 3.6 copy-start.23
  440.6 855.3 %all-reduce.7.cloned.1.call-start = ((), (), s32[]{:S(2)}) async-start(), calls=%async_computation.8 | async-start | bytes 56623104 | tf_op jit(solution)/shard_map/psum | solution.py:11
  537.2 3.5 copy-start.21
  537.2 3.5 copy-start.40
  540.6 1.9 copy-start.18
  542.6 3.9 copy-start.28
  542.6 3.9 copy-start.29
  542.6 3.9 copy-start.31
  542.6 3.9 copy-start.36
  542.6 3.9 copy-start.37
  632.7 4.7 copy-start.8
  632.7 4.7 copy-start.48
  1295.9 3.4 copy-start.14
  1299.3 2.5 copy-start.13
  1301.8 2.5 copy-start.12
  1304.3 10.7 slice-start.2
  1305.7 9.3 slice-start.3
  1305.7 9.3 slice-start.4
  (8 other events, 9.3 us)
Sparse Core Ops, SparseCore 0:
  440.7 94.3 all-reduce.8
  541.5 754.3 all-reduce.6
